TPU v7x, 32 devices: a whole 2x2x4 slice. The times are simulated.
32 devices in a mesh: groups: 2 (over y), region: 4 (over x, core), sub: 4 (over z).
Axes of the slice: x: 2, y: 2, z: 4, core: 2. Of those that a mesh axis runs over, the one named last changes fastest.
Arguments:
- node_latents: bfloat16 [4096, 512], P(('groups', 'region', 'sub')), parts along dimension 0, may hold values from -6 to 6
- edge_latents: bfloat16 [24576, 512], P(('groups', 'region', 'sub')), parts along dimension 0, may hold values from -6 to 6
- coarse_latents: bfloat16 [64, 512], P(('groups', 'region', 'sub')), parts along dimension 0, may hold values from -6 to 6
- node_cotangent: bfloat16 [4096, 512], P(('groups', 'region', 'sub')), parts along dimension 0, may hold values from -6 to 6
- edge_cotangent: bfloat16 [24576, 512], P(('groups', 'region', 'sub')), parts along dimension 0, may hold values from -6 to 6
- coarse_cotangent: bfloat16 [64, 512], P(('groups', 'region', 'sub')), parts along dimension 0, may hold values from -6 to 6
- edge_inner: bfloat16 [1536, 512], replicated, may hold values from -0.15625 to 0.15625
- edge_inner_bias: float32 [512], replicated, may hold values from -3 to 3
- edge_outer: bfloat16 [512, 512], replicated, may hold values from -0.25 to 0.25
- edge_outer_bias: float32 [512], replicated, may hold values from -3 to 3
- edge_gain: float32 [512], replicated, may hold values from 0.1 to 1.9
- node_inner: bfloat16 [1024, 512], replicated, may hold values from -0.1875 to 0.1875
- node_inner_bias: float32 [512], replicated, may hold values from -3 to 3
- node_outer: bfloat16 [512, 512], replicated, may hold values from -0.25 to 0.25
- node_outer_bias: float32 [512], replicated, may hold values from -3 to 3
- node_gain: float32 [512], replicated, may hold values from 0.1 to 1.9
- send_list: int32 [32, 8, 24], P(('groups', 'region', 'sub')), parts along dimension 0, may hold values from 0 to 127
- edge_sender: int32 [24576], P(('groups', 'region', 'sub')), parts along dimension 0, may hold values from 0 to 319
- edge_receiver: int32 [24576], P(('groups', 'region', 'sub')), parts along dimension 0, may hold values from 0 to 127
- coarse_sender: int32 [64], P('groups'), parts along dimension 0, may hold values from 0 to 15
- coarse_receiver: int32 [64], P('groups'), parts along dimension 0, may hold values from 0 to 15
Outputs:
- grad_nodes: bfloat16 [4096, 512], P(('groups', 'region', 'sub')), parts along dimension 0
- grad_edges: bfloat16 [24576, 512], P(('groups', 'region', 'sub')), parts along dimension 0
- grad_coarse: bfloat16 [64, 512], P(('groups', 'region', 'sub')), parts along dimension 0
- grad_edge_inner: float32 [3072, 512], P(('groups', 'region', 'sub')), parts along dimension 0
- grad_edge_outer: float32 [1024, 512], P(('groups', 'region', 'sub')), parts along dimension 0
- grad_node_inner: float32 [2048, 512], P(('groups', 'region', 'sub')), parts along dimension 0
- grad_node_outer: float32 [1024, 512], P(('groups', 'region', 'sub')), parts along dimension 0
There are 2 independent parts, one for each index of `groups`. A program takes and returns all parts, laid end to end along the dimension named above; an argument that names none is the same for every part. Nothing has to cross between parts.
Inputs may be any that keep to these rules, and one draw needn't show every extreme that they name: send_list[p, m, j] is a row of device p, sent to its neighbour at offset m as that neighbour's j-th row from it. `edge_sender`: below 128: a row of the edge's own device; 128 + m * 24 + j: the j-th row sent to it by its neighbour at the opposite of offset m. `edge_receiver`: a row of the edge's own device. `coarse_sender`: coarse node c is the first row of device c. `coarse_receiver`: numbered as coarse_sender.
All inputs are finite; a program needn't handle non-finite values.
Results may differ from a plain program's by a relative error of at most 0.0076.
Values may be sent and summed in bfloat16 or wider, within the bound.
A program may use at most 128 MiB of HBM per device.

v0:
```python
import jax
import jax.numpy as jnp
from jax import lax
from jax.sharding import PartitionSpec as P


def passed_along(value, axis, steps):
    count = lax.axis_size(axis)
    pairs = [(source, (source + steps) % count) for source in range(count)]
    return lax.ppermute(value, axis, pairs)


def for_sending(array):

    def short(part):
        return part.astype(jnp.bfloat16) if part.dtype == jnp.float32 else part

    return jax.tree.map(short, array)


def network_forward(inputs, inner, inner_bias, outer, outer_bias, gain):
    before = jnp.dot(inputs, inner, preferred_element_type=jnp.float32) + inner_bias
    hidden = jax.nn.silu(before).astype(jnp.bfloat16)
    after = jnp.dot(hidden, outer, preferred_element_type=jnp.float32) + outer_bias
    centred = after - jnp.mean(after, axis=-1, keepdims=True)
    inv_scale = lax.rsqrt(jnp.mean(centred * centred, axis=-1, keepdims=True) + 1e-05)
    normed = centred * inv_scale
    return (normed * gain, (before, hidden, normed, inv_scale))


def contract_rows(left, right):
    return lax.dot_general(
        left, right, (((0,), (0,)), ((), ())), preferred_element_type=jnp.float32
    )


def contract_cols(left, right):
    return lax.dot_general(
        left, right, (((1,), (1,)), ((), ())), preferred_element_type=jnp.float32
    )


def network_backward(upstream, inputs, inner, outer, gain, stored):
    before, hidden, normed, inv_scale = stored
    scaled = upstream * gain
    grad_after = inv_scale * (
        scaled
        - jnp.mean(scaled, axis=-1, keepdims=True)
        - normed * jnp.mean(scaled * normed, axis=-1, keepdims=True)
    )
    after_low = grad_after.astype(jnp.bfloat16)
    outer_grad = contract_rows(hidden, after_low)
    sigma = jax.nn.sigmoid(before)
    grad_before = contract_cols(after_low, outer) * sigma * (1.0 + before * (1.0 - sigma))
    before_low = grad_before.astype(jnp.bfloat16)
    inner_grad = contract_rows(inputs, before_low)
    input_grad = contract_cols(before_low, inner)
    return (input_grad, inner_grad, outer_grad)


def onehot_sum(targets, count, values):
    picker = (targets[None, :] == jnp.arange(count, dtype=jnp.int32)[:, None]).astype(jnp.float32)
    return jnp.dot(
        picker, values, preferred_element_type=jnp.float32, precision=lax.Precision.HIGHEST
    )


def with_centre(blocks):
    empty = jnp.zeros((1,) + blocks.shape[1:], blocks.dtype)
    grid = jnp.concatenate([blocks[:4], empty, blocks[4:]], axis=0)
    return grid.reshape((3, 3) + blocks.shape[1:])


def without_centre(grid):
    flat = grid.reshape((9,) + grid.shape[2:])
    return jnp.concatenate([flat[:4], flat[5:]], axis=0)


def per_device(
    node_latents,
    edge_latents,
    coarse_latents,
    node_cotangent,
    edge_cotangent,
    coarse_cotangent,
    edge_inner,
    edge_inner_bias,
    edge_outer,
    edge_outer_bias,
    edge_gain,
    node_inner,
    node_inner_bias,
    node_outer,
    node_outer_bias,
    node_gain,
    send_list,
    edge_sender,
    edge_receiver,
    coarse_sender,
    coarse_receiver,
):
    latent = node_latents.shape[1]
    local_rows = node_latents.shape[0]
    region_count = lax.axis_size("region")
    sub_count = lax.axis_size("sub")
    device_count = region_count * sub_count
    position = lax.axis_index(("region", "sub"))
    neighbours = send_list.shape[1]
    halo_rows = send_list.shape[2]
    send_rows = send_list[0].reshape(-1)
    outgoing = node_latents[send_rows].reshape(neighbours, halo_rows, latent)
    grid = with_centre(outgoing)
    region_moved = [passed_along(grid[step + 1], "region", step) for step in (-1, 1)]
    sectioned = jnp.stack([region_moved[0], grid[1], region_moved[1]], axis=0)
    sub_moved = [passed_along(sectioned[:, step + 1], "sub", step) for step in (-1, 1)]
    incoming = without_centre(jnp.stack([sub_moved[0], sectioned[:, 1], sub_moved[1]], axis=1))
    extended = jnp.concatenate(
        [node_latents, incoming.reshape(neighbours * halo_rows, latent)], axis=0
    )
    inputs = jnp.concatenate(
        [edge_latents, extended[edge_sender], node_latents[edge_receiver]], axis=1
    )
    message, edge_stored = network_forward(
        inputs, edge_inner, edge_inner_bias, edge_outer, edge_outer_bias, edge_gain
    )
    updated = (edge_latents.astype(jnp.float32) + message).astype(jnp.bfloat16)
    receive_low = (
        edge_receiver[None, :] == jnp.arange(local_rows, dtype=jnp.int32)[:, None]
    ).astype(jnp.bfloat16)
    summed = jnp.dot(receive_low, updated, preferred_element_type=jnp.float32)
    coarse_rows = 1
    coarse_edges = coarse_latents.shape[0]
    own_nodes = node_latents[:coarse_rows]
    coarse_nodes, coarse_edge_rows, coarse_upstream = (
        lax.all_gather(own_nodes, ("region", "sub"), axis=0, tiled=True),
        lax.all_gather(coarse_latents, ("region", "sub"), axis=0, tiled=True),
        lax.all_gather(coarse_cotangent, ("region", "sub"), axis=0, tiled=True),
    )
    coarse_inputs = jnp.concatenate(
        [coarse_edge_rows, coarse_nodes[coarse_sender], coarse_nodes[coarse_receiver]], axis=1
    )
    coarse_message, coarse_stored = network_forward(
        coarse_inputs, edge_inner, edge_inner_bias, edge_outer, edge_outer_bias, edge_gain
    )
    coarse_updated = (coarse_edge_rows.astype(jnp.float32) + coarse_message).astype(jnp.bfloat16)
    coarse_summed = jax.ops.segment_sum(
        coarse_updated.astype(jnp.float32), coarse_receiver, num_segments=device_count
    )
    coarse_own = lax.dynamic_slice_in_dim(coarse_summed, position * coarse_rows, coarse_rows)
    summed = summed.at[:coarse_rows].add(coarse_own)
    node_inputs = jnp.concatenate([node_latents, summed.astype(jnp.bfloat16)], axis=1)
    unused_out, node_stored = network_forward(
        node_inputs, node_inner, node_inner_bias, node_outer, node_outer_bias, node_gain
    )
    node_grad, node_inner_grad, node_outer_grad = network_backward(
        node_cotangent.astype(jnp.float32),
        node_inputs,
        node_inner,
        node_outer,
        node_gain,
        node_stored,
    )
    grad_nodes = node_cotangent.astype(jnp.float32) + node_grad[:, :latent]
    grad_summed = node_grad[:, latent:]
    total = edge_cotangent.astype(jnp.float32) + grad_summed[edge_receiver]
    edge_grad, fine_inner, fine_outer = network_backward(
        total, inputs, edge_inner, edge_outer, edge_gain, edge_stored
    )
    grad_edges = (total + edge_grad[:, :latent]).astype(jnp.bfloat16)
    extended_grads = onehot_sum(
        edge_sender, local_rows + neighbours * halo_rows, edge_grad[:, latent : 2 * latent]
    )
    grad_nodes = grad_nodes + extended_grads[:local_rows]
    grad_nodes = grad_nodes + onehot_sum(edge_receiver, local_rows, edge_grad[:, 2 * latent :])
    returning = extended_grads[local_rows:].reshape(neighbours, halo_rows, latent)
    back_grid = with_centre(returning)
    sub_back = [
        passed_along(back_grid[:, step + 1].astype(jnp.bfloat16), "sub", -step).astype(jnp.float32)
        for step in (-1, 1)
    ]
    sectioned_back = jnp.stack([sub_back[0], back_grid[:, 1], sub_back[1]], axis=1)
    region_back = [
        passed_along(for_sending(sectioned_back[step + 1]), "region", -step) for step in (-1, 1)
    ]
    returned = without_centre(
        jnp.stack([region_back[0], sectioned_back[1], region_back[1]], axis=0)
    )
    grad_nodes = grad_nodes + onehot_sum(
        send_rows, local_rows, returned.reshape(neighbours * halo_rows, latent)
    )
    coarse_needed = lax.all_gather(grad_summed[:coarse_rows], ("region", "sub"), axis=0, tiled=True)
    coarse_total = coarse_upstream.astype(jnp.float32) + coarse_needed[coarse_receiver]
    coarse_grad, coarse_inner, coarse_outer = network_backward(
        coarse_total, coarse_inputs, edge_inner, edge_outer, edge_gain, coarse_stored
    )
    coarse_edge_grads = (coarse_total + coarse_grad[:, :latent]).astype(jnp.bfloat16)
    coarse_node_grads = jax.ops.segment_sum(
        coarse_grad[:, latent : 2 * latent], coarse_sender, num_segments=device_count
    )
    coarse_node_grads = coarse_node_grads + jax.ops.segment_sum(
        coarse_grad[:, 2 * latent :], coarse_receiver, num_segments=device_count
    )
    grad_coarse = lax.dynamic_slice_in_dim(coarse_edge_grads, position * coarse_edges, coarse_edges)
    own_grads = lax.dynamic_slice_in_dim(coarse_node_grads, position * coarse_rows, coarse_rows)
    only_first = (position == 0).astype(jnp.float32)
    coarse_inner = coarse_inner * only_first
    coarse_outer = coarse_outer * only_first
    grad_nodes = grad_nodes.at[:coarse_rows].add(own_grads)
    weight_terms = (
        fine_inner + coarse_inner,
        fine_outer + coarse_outer,
        node_inner_grad,
        node_outer_grad,
    )
    reduced = (
        lax.psum_scatter(weight_terms[0], ("region", "sub"), scatter_dimension=0, tiled=True),
        lax.psum_scatter(weight_terms[1], ("region", "sub"), scatter_dimension=0, tiled=True),
        lax.psum_scatter(weight_terms[2], ("region", "sub"), scatter_dimension=0, tiled=True),
        lax.psum_scatter(weight_terms[3], ("region", "sub"), scatter_dimension=0, tiled=True),
    )
    return (
        grad_nodes.astype(jnp.bfloat16),
        grad_edges,
        grad_coarse,
        reduced[0],
        reduced[1],
        reduced[2],
        reduced[3],
    )


def solution(mesh):
    in_specs = (
        P(("groups", "region", "sub"), None),
        P(("groups", "region", "sub"), None),
        P(("groups", "region", "sub"), None),
        P(("groups", "region", "sub"), None),
        P(("groups", "region", "sub"), None),
        P(("groups", "region", "sub"), None),
        P(),
        P(),
        P(),
        P(),
        P(),
        P(),
        P(),
        P(),
        P(),
        P(),
        P(("groups", "region", "sub"), None, None),
        P(("groups", "region", "sub")),
        P(("groups", "region", "sub")),
        P("groups"),
        P("groups"),
    )
    out_specs = (
        P(("groups", "region", "sub"), None),
        P(("groups", "region", "sub"), None),
        P(("groups", "region", "sub"), None),
        P(("groups", "region", "sub"), None),
        P(("groups", "region", "sub"), None),
        P(("groups", "region", "sub"), None),
        P(("groups", "region", "sub"), None),
    )
    return jax.shard_map(
        per_device, mesh=mesh, in_specs=in_specs, out_specs=out_specs, check_vma=False
    )
```

profile of v0, /device:TPU:0, one launch (start us, length us, event | category | flops | bytes accessed | tf_op | source)
XLA Modules:
  0.0 401.4 jit_solution(5599158710993509243)
XLA Ops:
  8.2 2.0 gather_fusion
  10.2 2.4 collective-permute-start
  12.9 33.4 %all-gather.1 = bf16[16,1,512]{2,1,0:T(2,128)(2,1)S(1)} all-gather(bf16[1,1,512]{2,1,0:T(2,128)(2,1)S(1)} %slice_bitcast_fusion.8), channel_id=1, replica_groups=mesh['groups'=2,'region'=4,'sub'=4] {'region','sub'}, dimensions={0}, use_global_device_ids=true | all-gather | bytes 17408 | tf_op jit(solution)/shard_map/all_gather | solution.py:135
  46.3 28.6 %all-gather = bf16[16,2,512]{2,1,0:T(2,128)(2,1)S(1)} all-gather(bf16[1,2,512]{2,1,0:T(2,128)(2,1)S(1)} %bitcast.108), channel_id=1, replica_groups=mesh['groups'=2,'region'=4,'sub'=4] {'region','sub'}, dimensions={0}, use_global_device_ids=true | all-gather | bytes 34816 | tf_op jit(solution)/shard_map/all_gather | solution.py:136
  77.4 2.7 gather_fusion.2
  80.1 2.3 copy.55
  82.4 30.9 %all-gather.2 = bf16[16,2,512]{2,1,0:T(2,128)(2,1)S(1)} all-gather(bf16[1,2,512]{2,1,0:T(2,128)(2,1)S(1)} %bitcast.109), channel_id=1, replica_groups=mesh['groups'=2,'region'=4,'sub'=4] {'region','sub'}, dimensions={0}, use_global_device_ids=true | all-gather | bytes 34816 | tf_op jit(solution)/shard_map/all_gather | solution.py:137
  113.9 2.3 copy.58
  117.8 2.0 collective-permute-start.3
  119.8 2.2 constant_dynamic-update-slice_fusion.2
  124.1 3.3 gather_fusion.1
  127.4 2.1 constant_dynamic-update-slice_fusion.1
  130.5 3.1 fusion.55
  144.0 28.9 %all-gather.3 = f32[16,1,512]{2,1,0:T(1,128)S(1)} all-gather(f32[1,1,512]{2,1,0:T(1,128)S(1)} %slice_bitcast_fusion.7), channel_id=1, replica_groups=mesh['groups'=2,'region'=4,'sub'=4] {'region','sub'}, dimensions={0}, use_global_device_ids=true | all-gather | bytes 34816 | tf_op jit(solution)/shard_map/all_gather | solution.py:191
  175.5 3.1 gather_fusion.5
  178.6 1.9 copy.59
  180.6 2.2 multiply_reduce_fusion.2
  187.3 2.7 fusion.24
  192.8 2.9 multiply_convert_fusion
  197.2 2.3 fusion
  201.9 2.5 fusion.57
  204.5 2.1 copy-done.5
  208.0 3.0 copy.66
  211.0 2.8 add_convert_fusion
  213.8 2.3 copy.63
  216.2 2.6 fusion.3
  218.9 2.2 collective-permute-start.4
  222.8 2.1 fusion.5
  227.0 1.8 collective-permute-done.7
  231.6 28.4 %reduce-scatter.7.cloned.1.call-done = f32[32,512]{1,0:T(8,128)} async-done(((f32[512,512]{1,0:T(8,128)}), f32[32,512]{1,0:T(8,128)}) %reduce-scatter.7.cloned.1.call-update) | async-done | bytes 65552 | tf_op jit(solution)/shard_map/reduce_scatter | solution.py:217
  259.9 64.9 %reduce-scatter.9.cloned.1.call-done = f32[64,512]{1,0:T(8,128)} async-done(((f32[1024,512]{1,0:T(8,128)}), f32[64,512]{1,0:T(8,128)}) %reduce-scatter.9.cloned.1.call-update) | async-done | bytes 131088 | tf_op jit(solution)/shard_map/reduce_scatter | solution.py:218
  324.8 70.0 %reduce-scatter.5.cloned.1.call-done = f32[96,512]{1,0:T(8,128)} async-done(((f32[1536,512]{1,0:T(8,128)}), f32[96,512]{1,0:T(8,128)}) %reduce-scatter.5.cloned.1.call-update) | async-done | bytes 196624 | tf_op jit(solution)/shard_map/reduce_scatter | solution.py:216
  (247 shorter events, 40.2 us)
Async XLA Ops:
  7.2 69.1 %copy-start = (bf16[1536,512]{1,0:T(8,128)(2,1)S(1)}, bf16[1536,512]{1,0:T(8,128)(2,1)}, u32[]{:S(2)}) copy-start(bf16[1536,512]{1,0:T(8,128)(2,1)} %param.31) | copy-start | bytes 4718596
  7.2 5.5 %copy-start.1 = (bf16[128,512]{1,0:T(8,128)(2,1)S(1)}, bf16[128,512]{1,0:T(8,128)(2,1)}, u32[]{:S(2)}) copy-start(bf16[128,512]{1,0:T(8,128)(2,1)} %param.25) | copy-start | bytes 393220
  7.2 5.6 %copy-start.25 = (s32[768]{0:T(1024)S(1)}, s32[768]{0:T(1024)}, u32[]{:S(2)}) copy-start(s32[768]{0:T(1024)} %param.43) | copy-start | bytes 9220
  7.2 5.6 %copy-start.28 = (s32[768]{0:T(1024)S(1)}, s32[768]{0:T(1024)}, u32[]{:S(2)}) copy-start(s32[768]{0:T(1024)} %param.42) | copy-start | bytes 9220
  7.2 39.1 %copy-start.56 = (s32[32]{0:T(128)S(1)}, s32[32]{0:T(128)}, u32[]{:S(2)}) copy-start(s32[32]{0:T(128)} %param.44) | copy-start | bytes 388
  7.2 39.0 %copy-start.57 = (s32[32]{0:T(128)S(1)}, s32[32]{0:T(128)}, u32[]{:S(2)}) copy-start(s32[32]{0:T(128)} %param.45) | copy-start | bytes 388
  7.2 39.1 %copy-start.48 = (bf16[2,512]{1,0:T(2,128)(2,1)S(1)}, bf16[2,512]{1,0:T(2,128)(2,1)}, u32[]{:S(2)}) copy-start(bf16[2,512]{1,0:T(2,128)(2,1)} %param.27) | copy-start | bytes 6148
  7.3 224.3 %reduce-scatter.11.cloned.1.call-start = ((), (), s32[]{:S(2)}) async-start(), calls=%async_computation.7 | async-start | bytes 1114112 | tf_op jit(solution)/shard_map/reduce_scatter | solution.py:219
  8.2 68.1 %copy-start.44 = (f32[512]{0:T(512)S(1)}, f32[512]{0:T(512)}, u32[]{:S(2)}) copy-start(f32[512]{0:T(512)} %param.32) | copy-start | bytes 6148
  10.2 107.5 %collective-permute-start = (bf16[3,24,512]{2,1,0:T(8,128)(2,1)S(1)}, bf16[3,24,512]{2,1,0:T(8,128)(2,1)S(1)}, u32[]{:S(2)}, u32[]{:S(2)}) collective-permute-start(bf16[3,24,512]{2,1,0:T(8,128)(2,1)S(1)} %bitcast.106), channel_id=1, source_target_pairs={{0,12},{4,0},{8,4},{12,8},{1,13},{5,1},{9,5},{13,9},{2,14},{6,2},{... | collective-permute-start | bytes 221192 | tf_op jit(solution)/shard_map/ppermute | solution.py:10
  12.6 64.1 %copy-start.16 = (bf16[512,512]{1,0:T(8,128)(2,1)S(1)}, bf16[512,512]{1,0:T(8,128)(2,1)}, u32[]{:S(2)}) copy-start(bf16[512,512]{1,0:T(8,128)(2,1)} %param.33) | copy-start | bytes 1572868
  12.6 64.1 %copy-start.41 = (f32[512]{0:T(512)S(1)}, f32[512]{0:T(512)}, u32[]{:S(2)}) copy-start(f32[512]{0:T(512)} %param.34) | copy-start | bytes 6148
  12.6 105.1 %collective-permute-start.1 = (bf16[3,24,512]{2,1,0:T(8,128)(2,1)S(1)}, bf16[3,24,512]{2,1,0:T(8,128)(2,1)S(1)}, u32[]{:S(2)}, u32[]{:S(2)}) collective-permute-start(bf16[3,24,512]{2,1,0:T(8,128)(2,1)S(1)} %bitcast.105), channel_id=1, source_target_pairs={{0,4},{4,8},{8,12},{12,0},{1,5},{5,9},{9,13},{13,1},{2,6},{6,10},{... | collective-permute-start | bytes 221192 | tf_op jit(solution)/shard_map/ppermute | solution.py:10
  77.0 39.2 %copy-start.31 = (f32[32]{0:T(128)}, f32[32]{0:T(128)S(1)}, u32[]{:S(2)}) copy-start(f32[32]{0:T(128)S(1)} %broadcast_multiply_fusion.8) | copy-start | bytes 388
  77.3 39.0 %copy-start.36 = (f32[32]{0:T(128)}, f32[32]{0:T(128)S(1)}, u32[]{:S(2)}) copy-start(f32[32]{0:T(128)S(1)} %add_rsqrt_fusion.2) | copy-start | bytes 388
  80.1 36.2 %copy-start.24 = (f32[512]{0:T(512)S(1)}, f32[512]{0:T(512)}, u32[]{:S(2)}) copy-start(f32[512]{0:T(512)} %param.35) | copy-start | bytes 6148
  117.7 5.0 %collective-permute-start.2 = (bf16[3,24,512]{2,1,0:T(8,128)(2,1)S(1)}, bf16[3,24,512]{2,1,0:T(8,128)(2,1)S(1)}, u32[]{:S(2)}, u32[]{:S(2)}) collective-permute-start(bf16[3,24,512]{2,1,0:T(8,128)(2,1)S(1)} %get-tuple-element.76), channel_id=1, source_target_pairs={{0,3},{1,0},{2,1},{3,2},{4,7},{5,4},{6,5},{7,6},{8,11},{9,8},{10,9... | collective-permute-start | bytes 221192 | tf_op jit(solution)/shard_map/ppermute | solution.py:10
  117.8 6.2 %collective-permute-start.3 = (bf16[3,24,512]{2,1,0:T(8,128)(2,1)S(1)}, bf16[3,24,512]{2,1,0:T(8,128)(2,1)S(1)}, u32[]{:S(2)}, u32[]{:S(2)}) collective-permute-start(bf16[3,24,512]{2,1,0:T(8,128)(2,1)S(1)} %get-tuple-element.77), channel_id=1, source_target_pairs={{0,1},{1,2},{2,3},{3,0},{4,5},{5,6},{6,7},{7,4},{8,9},{9,10},{10,1... | collective-permute-start | bytes 221192 | tf_op jit(solution)/shard_map/ppermute | solution.py:10
  142.6 31.0 %copy-start.22 = (f32[32,512]{1,0:T(8,128)S(1)}, f32[32,512]{1,0:T(8,128)}, u32[]{:S(2)}) copy-start(f32[32,512]{1,0:T(8,128)} %reshape.299) | copy-start | bytes 196612
  142.6 31.0 %copy-start.32 = (f32[32]{0:T(128)S(1)}, f32[32]{0:T(128)}, u32[]{:S(2)}) copy-start(f32[32]{0:T(128)} %copy-done.31) | copy-start | bytes 388
  142.6 31.0 %copy-start.37 = (f32[32]{0:T(128)S(1)}, f32[32]{0:T(128)}, u32[]{:S(2)}) copy-start(f32[32]{0:T(128)} %copy-done.36) | copy-start | bytes 388
  143.1 32.4 %copy-start.27 = (s32[1024]{0:T(1024)S(1)}, s32[1024]{0:T(1024)}, u32[]{:S(2)}) copy-start(s32[1024]{0:T(1024)} %copy-done.26) | copy-start | bytes 12292
  144.0 116.0 %reduce-scatter.7.cloned.1.call-start = ((), (), s32[]{:S(2)}) async-start(), calls=%async_computation.5 | async-start | bytes 1114112 | tf_op jit(solution)/shard_map/reduce_scatter | solution.py:217
  187.0 137.8 %reduce-scatter.9.cloned.1.call-start = ((), (), s32[]{:S(2)}) async-start(), calls=%async_computation.6 | async-start | bytes 2228224 | tf_op jit(solution)/shard_map/reduce_scatter | solution.py:218
  190.1 204.8 %reduce-scatter.5.cloned.1.call-start = ((), (), s32[]{:S(2)}) async-start(), calls=%async_computation.4 | async-start | bytes 3342336 | tf_op jit(solution)/shard_map/reduce_scatter | solution.py:216
  200.0 4.4 %copy-start.10 = (f32[32,1536]{1,0:T(8,128)}, f32[32,1536]{1,0:T(8,128)S(1)}, u32[]{:S(2)}) copy-start(f32[32,1536]{1,0:T(8,128)S(1)} %fusion.58) | copy-start | bytes 589828
  218.7 4.1 %copy-start.9 = (f32[128,1024]{1,0:T(8,128)S(1)}, f32[128,1024]{1,0:T(8,128)}, u32[]{:S(2)}) copy-start(f32[128,1024]{1,0:T(8,128)} %copy-done.8) | copy-start | bytes 1572868
  218.9 6.1 %slice-start = ((f32[32,1536]{1,0:T(8,128)}), f32[32,512]{1,0:T(8,128)S(1)}, s32[]{:S(2)}) async-start(f32[32,1536]{1,0:T(8,128)} %copy-done.10), calls=%async_computation.8 | async-start | bytes 131072 | tf_op jit(solution)/shard_map/slice | solution.py:196
  218.9 7.3 %collective-permute-start.4 = (bf16[3,24,512]{2,1,0:T(8,128)(2,1)S(1)}, bf16[3,24,512]{2,1,0:T(8,128)(2,1)S(1)}, u32[]{:S(2)}, u32[]{:S(2)}) collective-permute-start(bf16[3,24,512]{2,1,0:T(8,128)(2,1)S(1)} %get-tuple-element.72), channel_id=1, source_target_pairs={{0,1},{1,2},{2,3},{3,0},{4,5},{5,6},{6,7},{7,4},{8,9},{9,10},{10,1... | collective-permute-start | bytes 221192 | tf_op jit(solution)/shard_map/ppermute | solution.py:10
  221.2 5.1 %collective-permute-start.5 = (bf16[3,24,512]{2,1,0:T(8,128)(2,1)S(1)}, bf16[3,24,512]{2,1,0:T(8,128)(2,1)S(1)}, u32[]{:S(2)}, u32[]{:S(2)}) collective-permute-start(bf16[3,24,512]{2,1,0:T(8,128)(2,1)S(1)} %get-tuple-element.73), channel_id=1, source_target_pairs={{0,3},{1,0},{2,1},{3,2},{4,7},{5,4},{6,5},{7,6},{8,11},{9,8},{10,9... | collective-permute-start | bytes 221192 | tf_op jit(solution)/shard_map/ppermute | solution.py:10
  226.4 2.5 collective-permute-start.7
  226.5 3.8 collective-permute-start.6
  (46 other events, 90.4 us)
Sparse Core Ops, SparseCore 0:
  144.1 54.7 reduce-scatter.10
  203.5 56.3 reduce-scatter.6
  264.3 60.5 reduce-scatter.8
  329.6 65.2 reduce-scatter.4
where the time goes:
time: 402 us; the launch traced here: 401 us
  waiting for transfers between devices  169 us (42%)
  blocking collectives  122 us (30%)
  local copies, waits for them, and re-layouts  42 us (10%)
  matrix products  29.8 us (7%)
  between operations  15 us (4%)
  other arithmetic  14.7 us (4%)
  starting transfers between devices  9.32 us (2%)
    reduce_scatter x1, waiting for transfers between devices, per_device(): lax.psum_scatter(weight_terms[0], ('region', 'sub'), scatter_dimension=0,...  70 us
    reduce_scatter x1, waiting for transfers between devices, per_device(): lax.psum_scatter(weight_terms[2], ('region', 'sub'), scatter_dimension=0,...  64.9 us
    all_gather x1, blocking collectives, per_device(): lax.all_gather(own_nodes, ('region', 'sub'), axis=0, tiled=True)  33.4 us
    all_gather x1, blocking collectives, per_device(): lax.all_gather(coarse_cotangent, ('region', 'sub'), axis=0, tiled=True)  30.9 us
    all_gather x1, blocking collectives, per_device(): lax.all_gather(grad_summed[:coarse_rows], ('region', 'sub'), axis=0, tile...  28.9 us
    all_gather x1, blocking collectives, per_device(): lax.all_gather(coarse_latents, ('region', 'sub'), axis=0, tiled=True)  28.6 us
    reduce_scatter x1, waiting for transfers between devices, per_device(): lax.psum_scatter(weight_terms[1], ('region', 'sub'), scatter_dimension=0,...  28.4 us
    unnamed x143, local copies, waits for them, and re-layouts  22.1 us
  transfers between devices with their start and end apart: 12, of which 7 were waited for; matrix products, arithmetic and copies ran while one was open for 15% of the time, Pallas kernels for 0%

commit v1 on v0

--- a/solution.py
+++ b/solution.py
@@ -1,6 +1,8 @@
 import jax
 import jax.numpy as jnp
 from jax import lax
+from jax.experimental import pallas as pl
+from jax.experimental.pallas import tpu as pltpu
 from jax.sharding import PartitionSpec as P
 
 
@@ -229,6 +231,475 @@
     )
 
 
+def dot(left, right):
+    return jnp.dot(left, right, preferred_element_type=jnp.float32)
+
+
+def one_hot(hits):
+    return jnp.where(hits, 1.0, 0.0).astype(jnp.bfloat16)
+
+
+def column_hot(row, first, count):
+    tall = jnp.transpose(jnp.broadcast_to(row, (128, row.shape[1])))
+    lanes = lax.broadcasted_iota(jnp.int32, tall.shape, 1)
+    parts = [one_hot(tall == lanes + (first + at)) for at in range(0, count, 128)]
+    return jnp.concatenate(parts, axis=1) if len(parts) > 1 else parts[0]
+
+
+def row_hot(row, count):
+    shape = (count, row.shape[1])
+    rows = lax.broadcasted_iota(jnp.int32, shape, 0)
+    return one_hot(jnp.broadcast_to(row, shape) == rows)
+
+
+def two_parts(value):
+    high = value.astype(jnp.bfloat16)
+    return high, (value - high.astype(jnp.float32)).astype(jnp.bfloat16)
+
+
+def layer_norm_parts(after):
+    centred = after - jnp.mean(after, axis=-1, keepdims=True)
+    inv_scale = lax.rsqrt(jnp.mean(centred * centred, axis=-1, keepdims=True) + 1e-05)
+    return centred * inv_scale, inv_scale
+
+
+def gradient_after(upstream, gain, normed, inv_scale):
+    scaled = upstream * gain
+    return inv_scale * (
+        scaled
+        - jnp.mean(scaled, axis=-1, keepdims=True)
+        - normed * jnp.mean(scaled * normed, axis=-1, keepdims=True)
+    )
+
+
+OFFSETS = ((-1, -1), (-1, 0), (-1, 1), (0, -1), (0, 1), (1, -1), (1, 0), (1, 1))
+SLOT = 32
+SIDE = 4
+DEVICES = SIDE * SIDE
+FINE = 768
+ROWS = 896
+OWN = 128
+EXTENDED = OWN + 8 * SLOT
+PIECES = ((0, 256), (256, 256), (512, 256), (768, 128))
+CHUNKS = ((96, 512), (32, 512), (96, 256), (96, 256))
+
+
+def step_kernel(
+    index_ref, params_ref, packet_ref,
+    nodes_ref, edges_ref, node_cot_ref, edge_cot_ref,
+    w1_ref, w2_ref, v1_ref, v2_ref,
+    grad_nodes_ref, grad_edges_ref, grad_coarse_ref,
+    out_ei_ref, out_eo_ref, out_ni_ref, out_no_ref,
+    joined, ext, outgoing, coarse_tiles, before_ref, hidden_ref, normed_ref, inv_ref,
+    updated_ref, after_low_ref, before_low_ref, masked, send_back, returned,
+    coarse_cot, coarse_sums,
+    g0, g1, g2, g3, a0, a1, a2, a3, b0, b1, b2, b3, c0, c1, c2, c3,
+    t0, t1, t2, t3, d0, d1, d2, d3, e0, e1, e2, e3,
+    halo_send, halo_recv, coarse_send, coarse_recv, sums_send, sums_recv,
+    back_send, back_recv, s1_send, s1_recv, s2_send, s2_recv, s3_send, s3_recv,
+):
+    bf16, f32 = jnp.bfloat16, jnp.float32
+    group = lax.axis_index("groups")
+    region = lax.axis_index("region")
+    sub = lax.axis_index("sub")
+    position = region * SIDE + sub
+    core = lax.rem(region, 2)
+    column = lax.div(region, 2)
+
+    def at(r, s):
+        return (group, lax.rem(r + SIDE, SIDE), lax.rem(s + SIDE, SIDE))
+
+    def flat(k):
+        other = lax.rem(position + k + DEVICES, DEVICES)
+        return other, (group, lax.div(other, SIDE), lax.rem(other, SIDE))
+
+    def remote(src, dst, send, recv, device):
+        return pltpu.make_async_remote_copy(
+            src_ref=src, dst_ref=dst, send_sem=send, recv_sem=recv,
+            device_id=device, device_id_type=pl.DeviceIdType.MESH,
+        )
+
+    barrier = pltpu.get_barrier_semaphore()
+    for k in range(1, DEVICES):
+        pl.semaphore_signal(
+            barrier, inc=1, device_id=flat(k)[1], device_id_type=pl.DeviceIdType.MESH
+        )
+    nodes = nodes_ref[...]
+    send_row = index_ref[:, 1792:2048]
+    outgoing[...] = dot(column_hot(send_row, 0, OWN), nodes).astype(bf16)
+    coarse_tiles[position] = packet_ref[...]
+    ext[0:OWN, :] = nodes
+    pl.semaphore_wait(barrier, DEVICES - 1)
+
+    waits = []
+    halo = []
+    for m, (dr, ds) in enumerate(OFFSETS):
+        slot = pl.ds(OWN + m * SLOT, SLOT)
+        copy = remote(
+            outgoing.at[pl.ds(m * SLOT, SLOT)], ext.at[slot],
+            halo_send.at[m], halo_recv.at[m], at(region + dr, sub + ds),
+        )
+        copy.start()
+        halo.append(copy)
+    coarse = []
+    for k in range(1, DEVICES):
+        _, device = flat(k)
+        sender, _ = flat(-k)
+        remote(
+            coarse_tiles.at[position], coarse_tiles.at[position],
+            coarse_send.at[k], coarse_recv.at[k], device,
+        ).start()
+        coarse.append(remote(
+            coarse_tiles.at[position], coarse_tiles.at[sender],
+            coarse_send.at[k], coarse_recv.at[k], device,
+        ))
+
+    b1_row, b2_row, gain = params_ref[0:1, :], params_ref[1:2, :], params_ref[2:3, :]
+    c1_row, c2_row, node_gain = params_ref[3:4, :], params_ref[4:5, :], params_ref[5:6, :]
+
+    for first, size in PIECES[:3]:
+        rows = pl.ds(first, size)
+        joined[rows, 0:512] = edges_ref[rows, :]
+        masked[rows, :] = edges_ref[rows, :]
+        picker = column_hot(index_ref[:, 896 + first:896 + first + size], 0, OWN)
+        joined[rows, 1024:1536] = dot(picker, nodes).astype(bf16)
+    for copy in halo:
+        copy.wait()
+    extended = ext[...]
+    for first, size in PIECES[:3]:
+        rows = pl.ds(first, size)
+        picker = column_hot(index_ref[:, first:first + size], 0, EXTENDED)
+        joined[rows, 512:1024] = dot(picker, extended).astype(bf16)
+
+    piece_rows = lax.broadcasted_iota(jnp.int32, (128, 1), 0)
+    is_own = (piece_rows >= 2 * position) & (piece_rows < 2 * position + 2)
+    own_mask = jnp.where(is_own, 1.0, 0.0)
+
+    for first, size in PIECES:
+        rows = pl.ds(first, size)
+        if first == FINE:
+            for copy in coarse:
+                copy.wait()
+            table = coarse_tiles[...].reshape(DEVICES * 16, 512)
+            picked = dot(column_hot(index_ref[:, 2048:2176], 0, DEVICES * 16), table)
+            blank = jnp.zeros((96, 512), f32)
+
+            def placed(part):
+                return jnp.concatenate([part, blank], axis=0)
+
+            latents = placed(picked[0:32])
+            joined[rows, 0:512] = latents.astype(bf16)
+            joined[rows, 512:1024] = placed(picked[32:64]).astype(bf16)
+            joined[rows, 1024:1536] = placed(picked[64:96]).astype(bf16)
+            masked[rows, :] = (latents * own_mask).astype(bf16)
+            coarse_cot[...] = placed(picked[96:128])
+        before = dot(joined[rows, :], w1_ref[...]) + b1_row
+        before_ref[rows, :] = before
+        hidden = (before * jax.nn.sigmoid(before)).astype(bf16)
+        hidden_ref[rows, :] = hidden
+        after = dot(hidden, w2_ref[...]) + b2_row
+        normed, inv_scale = layer_norm_parts(after)
+        normed_ref[rows, :] = normed
+        inv_ref[rows, :] = jnp.broadcast_to(inv_scale, (size, 128))
+        updated_ref[rows, :] = (joined[rows, 0:512].astype(f32) + normed * gain).astype(bf16)
+    coarse_rows = pl.ds(FINE, 128)
+    hidden_ref[coarse_rows, :] = (hidden_ref[coarse_rows, :].astype(f32) * own_mask).astype(bf16)
+
+    to_receiver = row_hot(index_ref[:, 896:1792], OWN)
+    summed = dot(to_receiver, updated_ref[...])
+
+    summed_low = summed.astype(bf16)
+    node_before = dot(nodes, v1_ref[0:512, :]) + dot(summed_low, v1_ref[512:1024, :]) + c1_row
+    sigma = jax.nn.sigmoid(node_before)
+    node_hidden = (node_before * sigma).astype(bf16)
+    node_normed, node_inv = layer_norm_parts(dot(node_hidden, v2_ref[...]) + c2_row)
+    node_cot = node_cot_ref[...].astype(f32)
+    node_after = gradient_after(node_cot, node_gain, node_normed, node_inv).astype(bf16)
+    node_low = (
+        contract_cols(node_after, v2_ref[...]) * sigma * (1.0 + node_before * (1.0 - sigma))
+    ).astype(bf16)
+    grad_summed = contract_cols(node_low, v1_ref[512:1024, :])
+    for part in range(4):
+        coarse_sums[position, part:part + 1, :] = grad_summed[0:1, 128 * part:128 * part + 128]
+    sums = []
+    for k in range(1, DEVICES):
+        _, device = flat(k)
+        sender, _ = flat(-k)
+        remote(
+            coarse_sums.at[position], coarse_sums.at[position],
+            sums_send.at[k], sums_recv.at[k], device,
+        ).start()
+        sums.append(remote(
+            coarse_sums.at[position], coarse_sums.at[sender],
+            sums_send.at[k], sums_recv.at[k], device,
+        ))
+
+    grads, mine, passing, crossed = (g0, g1, g2, g3), (a0, a1, a2, a3), (b0, b1, b2, b3), (c0, c1, c2, c3)
+    totals, along, arrived = (t0, t1, t2, t3), (d0, d1, d2, d3), (e0, e1, e2, e3)
+    partner_core = (group, column * 2 + (1 - core), sub)
+    partner_column = (group, (1 - column) * 2 + core, sub)
+
+    def core_copy(n, which):
+        return remote(
+            grads[n].at[which * 2 + (1 - core)], mine[n].at[which],
+            s1_send.at[n, which], s1_recv.at[n, which], partner_core,
+        )
+
+    def start_core(n):
+        core_copy(n, 1 - column).start()
+        core_copy(n, column).start()
+
+    def column_copy(n):
+        return remote(passing[n], crossed[n], s2_send.at[n], s2_recv.at[n], partner_column)
+
+    def start_column(n):
+        core_copy(n, 1 - column).wait()
+        passing[n][...] = (
+            grads[n][(1 - column) * 2 + core].astype(f32) + mine[n][1 - column].astype(f32)
+        ).astype(bf16)
+        column_copy(n).start()
+
+    def total_column(n):
+        core_copy(n, column).wait()
+        column_copy(n).wait()
+        totals[n][...] = (
+            grads[n][column * 2 + core].astype(f32)
+            + mine[n][column].astype(f32)
+            + crossed[n][...].astype(f32)
+        )
+
+    def line_copy(n, way, block):
+        step = 1 if way == 0 else SIDE - 1
+        return remote(
+            along[n].at[way, block], arrived[n].at[way, block],
+            s3_send.at[n, way, block], s3_recv.at[n, way, block],
+            (group, region, lax.rem(sub + step, SIDE)),
+        )
+
+    def line_step(n, k):
+        for way, block, first, sends in (
+            (0, 3 - k, 0, sub < 3 - k), (1, k, SIDE - 1, sub > k)
+        ):
+            @pl.when(sends & (sub == first))
+            def _():
+                along[n][way, block] = totals[n][block].astype(bf16)
+                line_copy(n, way, block).start()
+
+            @pl.when(sends & (sub != first))
+            def _():
+                line_copy(n, way, block).wait_recv()
+                along[n][way, block] = (
+                    totals[n][block] + arrived[n][way, block].astype(f32)
+                ).astype(bf16)
+                line_copy(n, way, block).start()
+
+    def line_end(n):
+        @pl.when(sub > 0)
+        def _():
+            line_copy(n, 0, sub).wait_recv()
+            totals[n][sub] = totals[n][sub] + arrived[n][0, sub].astype(f32)
+
+        @pl.when(sub < SIDE - 1)
+        def _():
+            line_copy(n, 1, sub).wait_recv()
+            totals[n][sub] = totals[n][sub] + arrived[n][1, sub].astype(f32)
+
+        for k in range(SIDE - 1):
+            @pl.when(sub < 3 - k)
+            def _():
+                line_copy(n, 0, 3 - k).wait_send()
+
+            @pl.when(sub > k)
+            def _():
+                line_copy(n, 1, k).wait_send()
+        return totals[n][sub]
+
+    node_inner_grad = jnp.concatenate(
+        [contract_rows(nodes, node_low), contract_rows(summed_low, node_low)], axis=0
+    ).astype(bf16)
+    node_outer_grad = contract_rows(node_hidden, node_after).astype(bf16)
+    g0[:, :, 0:64, :] = node_inner_grad.reshape(SIDE, SIDE, 64, 512)
+    g0[:, :, 64:96, :] = node_outer_grad.reshape(SIDE, SIDE, 32, 512)
+    start_core(0)
+    node_direct = node_cot + contract_cols(node_low, v1_ref[0:512, :])
+
+    sums_high, sums_low = two_parts(grad_summed)
+    for first, size in PIECES:
+        rows = pl.ds(first, size)
+        if first == FINE:
+            for copy in sums:
+                copy.wait()
+            gathered = jnp.concatenate([coarse_sums[:, part, :] for part in range(4)], axis=1)
+            gathered = jnp.concatenate([gathered, jnp.zeros((OWN - DEVICES, 512), f32)], axis=0)
+            high, low = two_parts(gathered)
+            picker = column_hot(index_ref[:, 2176:2304], 0, OWN)
+            total = coarse_cot[...] + (dot(picker, high) + dot(picker, low))
+        else:
+            picker = column_hot(index_ref[:, 896 + first:896 + first + size], 0, OWN)
+            total = edge_cot_ref[rows, :].astype(f32) + (dot(picker, sums_high) + dot(picker, sums_low))
+        after_low = gradient_after(
+            total, gain, normed_ref[rows, :], inv_ref[rows, 0:1]
+        ).astype(bf16)
+        after_low_ref[rows, :] = after_low
+        before = before_ref[rows, :]
+        sigma = jax.nn.sigmoid(before)
+        before_low = (
+            contract_cols(after_low, w2_ref[...]) * sigma * (1.0 + before * (1.0 - sigma))
+        ).astype(bf16)
+        before_low_ref[rows, :] = before_low
+        direct = total + contract_cols(before_low, w1_ref[0:512, :])
+        if first == FINE:
+            row_pair = [
+                jnp.sum(jnp.where(piece_rows == 2 * position + j, direct, 0.0), axis=0, keepdims=True)
+                for j in range(2)
+            ]
+            is_second = lax.broadcasted_iota(jnp.int32, (2, 512), 0) == 1
+            grad_coarse_ref[...] = jnp.where(is_second, row_pair[1], row_pair[0]).astype(bf16)
+        else:
+            grad_edges_ref[rows, :] = direct.astype(bf16)
+        if first == 256:
+            start_column(0)
+
+    g1[...] = contract_rows(hidden_ref[...], after_low_ref[...]).astype(bf16).reshape(g1.shape)
+    start_core(1)
+    to_sender = row_hot(index_ref[:, 0:896], EXTENDED)
+    from_high, from_low = two_parts(dot(to_sender, before_low_ref[...]))
+    to_high, to_low = two_parts(dot(to_receiver, before_low_ref[...]))
+    w1b, w1c = w1_ref[512:1024, :], w1_ref[1024:1536, :]
+    from_grads = contract_cols(from_high, w1b) + contract_cols(from_low, w1b)
+    send_back[...] = from_grads[OWN:].astype(bf16)
+    back = []
+    for m, (dr, ds) in enumerate(OFFSETS):
+        slot = pl.ds(m * SLOT, SLOT)
+        copy = remote(
+            send_back.at[slot], returned.at[slot],
+            back_send.at[m], back_recv.at[m], at(region - dr, sub - ds),
+        )
+        copy.start()
+        back.append(copy)
+    start_column(1)
+    for n, buffer in ((2, g2), (3, g3)):
+        cols = slice(256 * (n - 2), 256 * (n - 2) + 256)
+        inner = jnp.concatenate([
+            contract_rows(masked[...], before_low_ref[:, cols]),
+            contract_rows(extended, from_high[:, cols]) + contract_rows(extended, from_low[:, cols]),
+            contract_rows(nodes, to_high[:, cols]) + contract_rows(nodes, to_low[:, cols]),
+        ], axis=0)
+        buffer[...] = inner.astype(bf16).reshape(buffer.shape)
+        start_core(n)
+        if n == 2:
+            total_column(0)
+            line_step(0, 0)
+    start_column(2)
+    line_step(0, 1)
+    start_column(3)
+    own = node_direct + from_grads[0:OWN]
+    own = own + (contract_cols(to_high, w1c) + contract_cols(to_low, w1c))
+    line_step(0, 2)
+    for copy in back:
+        copy.wait()
+    own = own + dot(row_hot(send_row, OWN), returned[...])
+    grad_nodes_ref[...] = own.astype(bf16)
+    total_column(1)
+    line_step(1, 0)
+    line_step(1, 1)
+    line_step(1, 2)
+    total_column(2)
+    line_step(2, 0)
+    node_block = line_end(0)
+    out_ni_ref[...] = node_block[0:64]
+    out_no_ref[...] = node_block[64:96]
+    line_step(2, 1)
+    total_column(3)
+    line_step(3, 0)
+    line_step(2, 2)
+    line_step(3, 1)
+    out_eo_ref[...] = line_end(1)
+    line_step(3, 2)
+    out_ei_ref[:, 0:256] = line_end(2)
+    out_ei_ref[:, 256:512] = line_end(3)
+
+
+def fused_device(
+    node_latents, edge_latents, coarse_latents, node_cotangent, edge_cotangent, coarse_cotangent,
+    edge_inner, edge_inner_bias, edge_outer, edge_outer_bias, edge_gain,
+    node_inner, node_inner_bias, node_outer, node_outer_bias, node_gain,
+    send_list, edge_sender, edge_receiver, coarse_sender, coarse_receiver,
+):
+    bf16, f32, dma = jnp.bfloat16, jnp.float32, pltpu.SemaphoreType.DMA
+    position = lax.axis_index("region") * SIDE + lax.axis_index("sub")
+    halo_slot = jnp.maximum(edge_sender - OWN, 0) // send_list.shape[2]
+    padded_sender = edge_sender + halo_slot * (SLOT - send_list.shape[2])
+    none = jnp.full((96,), -1, jnp.int32)
+    every = jnp.arange(2 * DEVICES, dtype=jnp.int32)
+    tile_row = 16 * (every // 2) + every % 2
+    index = jnp.concatenate([
+        padded_sender, jnp.where(coarse_sender == position, 0, -1), none,
+        edge_receiver, jnp.where(coarse_receiver == position, 0, -1), none,
+        jnp.pad(send_list[0], ((0, 0), (0, SLOT - send_list.shape[2])), constant_values=-1).reshape(-1),
+        tile_row + 1, 16 * coarse_sender, 16 * coarse_receiver, tile_row + 3,
+        coarse_receiver, none,
+    ]).reshape(1, -1)
+    blank = jnp.zeros((512,), f32)
+    params = jnp.stack([
+        edge_inner_bias, edge_outer_bias, edge_gain,
+        node_inner_bias, node_outer_bias, node_gain, blank, blank,
+    ])
+    packet = jnp.concatenate(
+        [node_latents[:1], coarse_latents, coarse_cotangent, jnp.zeros((11, 512), bf16)], axis=0
+    )
+
+    def per_chunk(make):
+        return [pltpu.VMEM(*make(rows, cols)) for rows, cols in CHUNKS]
+
+    scratch = [
+        pltpu.VMEM((ROWS, 1536), bf16),
+        pltpu.VMEM((EXTENDED, 512), bf16),
+        pltpu.VMEM((8 * SLOT, 512), bf16),
+        pltpu.VMEM((DEVICES, 16, 512), bf16),
+        pltpu.VMEM((ROWS, 512), f32),
+        pltpu.VMEM((ROWS, 512), bf16),
+        pltpu.VMEM((ROWS, 512), f32),
+        pltpu.VMEM((ROWS, 128), f32),
+        pltpu.VMEM((ROWS, 512), bf16),
+        pltpu.VMEM((ROWS, 512), bf16),
+        pltpu.VMEM((ROWS, 512), bf16),
+        pltpu.VMEM((ROWS, 512), bf16),
+        pltpu.VMEM((8 * SLOT, 512), bf16),
+        pltpu.VMEM((8 * SLOT, 512), bf16),
+        pltpu.VMEM((128, 512), f32),
+        pltpu.VMEM((DEVICES, 4, 128), f32),
+        *per_chunk(lambda n, c: ((SIDE, SIDE, n, c), bf16)),
+        *per_chunk(lambda n, c: ((2, SIDE, n, c), bf16)),
+        *per_chunk(lambda n, c: ((SIDE, n, c), bf16)),
+        *per_chunk(lambda n, c: ((SIDE, n, c), bf16)),
+        *per_chunk(lambda n, c: ((SIDE, n, c), f32)),
+        *per_chunk(lambda n, c: ((2, SIDE, n, c), bf16)),
+        *per_chunk(lambda n, c: ((2, SIDE, n, c), bf16)),
+        dma((8,)), dma((8,)), dma((DEVICES,)), dma((DEVICES,)), dma((DEVICES,)), dma((DEVICES,)),
+        dma((8,)), dma((8,)), dma((4, 2)), dma((4, 2)), dma((4,)), dma((4,)),
+        dma((4, 2, SIDE)), dma((4, 2, SIDE)),
+    ]
+    shape = jax.ShapeDtypeStruct
+    vmem = pl.BlockSpec(memory_space=pltpu.VMEM)
+    return pl.pallas_call(
+        step_kernel,
+        out_shape=(
+            shape((OWN, 512), bf16), shape((FINE, 512), bf16), shape((2, 512), bf16),
+            shape((96, 512), f32), shape((32, 512), f32), shape((64, 512), f32), shape((32, 512), f32),
+        ),
+        in_specs=[vmem] * 11,
+        out_specs=(vmem,) * 7,
+        scratch_shapes=scratch,
+        compiler_params=pltpu.CompilerParams(
+            collective_id=0, has_side_effects=True, vmem_limit_bytes=58 * 2**20
+        ),
+    )(
+        index, params, packet, node_latents, edge_latents, node_cotangent, edge_cotangent,
+        edge_inner, edge_outer, node_inner, node_outer,
+    )
+
+
 def solution(mesh):
     in_specs = (
         P(("groups", "region", "sub"), None),
@@ -262,6 +733,7 @@
         P(("groups", "region", "sub"), None),
         P(("groups", "region", "sub"), None),
     )
+    small = mesh.shape["region"] == SIDE and mesh.shape["sub"] == SIDE
     return jax.shard_map(
-        per_device, mesh=mesh, in_specs=in_specs, out_specs=out_specs, check_vma=False
-    )
+        fused_device if small else per_device, mesh=mesh, in_specs=in_specs, out_specs=out_specs, check_vma=False
+    )

time: 402 us -> 90.9 us (0.23)
  waiting for transfers between devices: 169 us -> 0 us
  blocking collectives: 122 us -> 0 us
  Pallas kernels: 0 us -> 75.9 us
  local copies, waits for them, and re-layouts: 42 us -> 11.2 us
  matrix products: 29.8 us -> 0 us
  between operations: 15 us -> 0.71 us
  other arithmetic: 14.7 us -> 2.76 us
  starting transfers between devices: 9.32 us -> 0 us
    reduce_scatter x4 -> x0, waiting for transfers between devices: 163 us -> none  [the longest x1 70 us: per_device(): lax.psum_scatter(weight_terms[0], ('region', 'sub'), scatter_dimension=0,...]
    all_gather x4 -> x0, blocking collectives: 122 us -> none  [the longest x1 33.4 us: per_device(): lax.all_gather(own_nodes, ('region', 'sub'), axis=0, tiled=True)]
    pallas_call x0 -> x1, Pallas kernels: none -> 75.9 us  [fused_device(): pl.pallas_call(step_kernel, out_shape=(shape((OWN, 512), bf16), shape((FI...]
    dot_general x22 -> x0, matrix products: 29.8 us -> none  [the longest x6 9.81 us: contract_rows(): lax.dot_general(left, right, (((0,), (0,)), ((), ())), preferred_element_...]
    unnamed x143 -> x17, local copies, waits for them, and re-layouts: 22.1 us -> 6.88 us
    gather x8 -> x0, local copies, waits for them, and re-layouts: 14.9 us -> none  [the longest x2 4.98 us: per_device(): total = edge_cotangent.astype(jnp.float32) + grad_summed[edge_receiver]]
    ppermute x8 -> x0, starting transfers between devices: 8.98 us -> none  [passed_along(): return lax.ppermute(value, axis, pairs)]
    convert_element_type x5 -> x0, other arithmetic: 5.36 us -> none  [the longest x1 2.82 us: per_device(): grad_edges = (total + edge_grad[:, :latent]).astype(jnp.bfloat16)]
  transfers between devices with their start and end apart: 12 -> 0, of which waited for: 7 -> 0; matrix products, arithmetic and copies ran while one was open for 15% -> 0% of each run, Pallas kernels for 0% -> 0%
where the time goes in v1:
time: 90.9 us; the launch traced here: 90.5 us
  Pallas kernels  75.9 us (83%)
  local copies, waits for them, and re-layouts  11.2 us (12%)
  other arithmetic  2.76 us (3%)
    pallas_call x1, Pallas kernels, fused_device(): pl.pallas_call(step_kernel, out_shape=(shape((OWN, 512), bf16), shape((FI...  75.9 us
    unnamed x17, local copies, waits for them, and re-layouts  6.88 us

profile of v1, /device:TPU:0, one launch (start us, length us, event | category | flops | bytes accessed | tf_op | source)
XLA Modules:
  0.0 90.5 jit_solution(12675387744725010974)
XLA Ops:
  0.6 0.1 pad.8.clone
  0.7 0.7 broadcast_multiply_fusion
  1.4 0.7 slice.3
  2.1 0.7 pad.4
  2.8 0.1 reshape.20
  2.9 0.7 fusion.1
  3.6 0.8 concatenate.6
  4.4 0.6 reshape.21.index_ref
  5.0 1.4 %stack.31.params_ref = f32[8,512]{1,0:T(8,128)} concatenate(f32[1,512]{1,0:T(1,128)} %bitcast.8, f32[1,512]{1,0:T(1,128)} %bitcast.9, f32[1,512]{1,0:T(1,128)} %bitcast.10, f32[1,512]{1,0:T(1,128)} %bitcast.11, f32[1,512]{1,0:T(1,128)} %bitcast.12, f32[1,512]{1,0:T(1,128)} %bitcast.13, f32[2,512]{1,0:T(2,128)S(1)} %stack.30), dimensions={0} | concatenate | bytes 32768 | tf_op jit(solution)/shard_map/stack | solution.py:644
  6.4 1.4 %maximum_maximum_fusion.packet_ref = bf16[16,512]{1,0:T(8,128)(2,1)} fusion(bf16[2,512]{1,0:T(2,128)(2,1)} %param.26, bf16[2,512]{1,0:T(2,128)(2,1)} %param.23, bf16[1,512]{1,0:T(2,128)(2,1)S(1)} %slice.3, bf16[16]{0:T(256)(128)(2,1)S(1)} %pad.8.clone), kind=kLoop, calls=%fused_computation | loop fusion | flops 65536 | bytes 21536 | tf_op jit(solution)/shard_map/concatenate | solution.py:648
  7.7 75.9 %shard_map.252 = (bf16[128,512]{1,0:T(8,128)(2,1)}, bf16[768,512]{1,0:T(8,128)(2,1)}, bf16[2,512]{1,0:T(2,128)(2,1)}, f32[96,512]{1,0:T(8,128)}, f32[32,512]{1,0...) custom-call(s32[1,2304]{1,0:T(1,128)} %reshape.21.index_ref, f32[8,512]{1,0:T(8,128)} %stack.31.params_ref, ...), custom_call_target="tpu_custom_call" | custom-call | tf_op jit(solution)/shard_map/pallas_call | solution.py:685
  83.6 0.0 copy-start.4
  83.6 0.0 copy-start
  83.6 0.0 copy-start.3
  83.6 0.0 copy-start.1
  83.7 0.0 copy-start.2
  83.7 1.6 %copy.35 = bf16[128,512]{1,0:T(8,128)(2,1)} copy(bf16[128,512]{1,0:T(8,128)(2,1)} %get-tuple-element.22) | data formatting | bytes 262144
  85.3 2.1 %copy.36 = bf16[768,512]{1,0:T(8,128)(2,1)} copy(bf16[768,512]{1,0:T(8,128)(2,1)} %get-tuple-element.23) | data formatting | bytes 1572864
  87.4 0.0 copy-done.4
  87.4 0.6 copy.37
  87.9 0.0 copy-done
  87.9 0.7 copy.38
  88.6 0.0 copy-done.3
  88.6 0.6 copy.39
  89.3 0.0 copy-done.1
  89.3 0.7 copy.40
  89.9 0.0 copy-done.2
  89.9 0.6 copy.41
  (4 shorter events, 0.0 us)
Async XLA Ops:
  83.6 3.7 %copy-start.4 = (bf16[2,512]{1,0:T(2,128)(2,1)S(1)}, bf16[2,512]{1,0:T(2,128)(2,1)}, u32[]{:S(2)}) copy-start(bf16[2,512]{1,0:T(2,128)(2,1)} %get-tuple-element.24) | copy-start | bytes 6148
  83.6 4.3 %copy-start = (f32[96,512]{1,0:T(8,128)S(1)}, f32[96,512]{1,0:T(8,128)}, u32[]{:S(2)}) copy-start(f32[96,512]{1,0:T(8,128)} %get-tuple-element.25) | copy-start | bytes 589828
  83.6 5.0 %copy-start.3 = (f32[32,512]{1,0:T(8,128)S(1)}, f32[32,512]{1,0:T(8,128)}, u32[]{:S(2)}) copy-start(f32[32,512]{1,0:T(8,128)} %get-tuple-element.26) | copy-start | bytes 196612
  83.6 5.6 %copy-start.1 = (f32[64,512]{1,0:T(8,128)S(1)}, f32[64,512]{1,0:T(8,128)}, u32[]{:S(2)}) copy-start(f32[64,512]{1,0:T(8,128)} %get-tuple-element.27) | copy-start | bytes 393220
  83.7 6.3 %copy-start.2 = (f32[32,512]{1,0:T(8,128)S(1)}, f32[32,512]{1,0:T(8,128)}, u32[]{:S(2)}) copy-start(f32[32,512]{1,0:T(8,128)} %get-tuple-element.28) | copy-start | bytes 196612

commit v2 on v1

--- a/solution.py
+++ b/solution.py
@@ -286,10 +286,10 @@
 
 def step_kernel(
     index_ref, params_ref, packet_ref,
-    nodes_ref, edges_ref, node_cot_ref, edge_cot_ref,
-    w1_ref, w2_ref, v1_ref, v2_ref,
+    nodes_ref, edges_hbm, node_cot_ref, edge_cot_hbm, w1_hbm, w2_hbm, v1_hbm, v2_hbm,
     grad_nodes_ref, grad_edges_ref, grad_coarse_ref,
     out_ei_ref, out_eo_ref, out_ni_ref, out_no_ref,
+    edges_ref, edge_cot_ref, w1_ref, w2_ref, v1_ref, v2_ref, load_sems,
     joined, ext, outgoing, coarse_tiles, before_ref, hidden_ref, normed_ref, inv_ref,
     updated_ref, after_low_ref, before_low_ref, masked, send_back, returned,
     coarse_cot, coarse_sums,
@@ -319,11 +319,20 @@
             device_id=device, device_id_type=pl.DeviceIdType.MESH,
         )
 
+    loads = [
+        pltpu.make_async_copy(src, dst, load_sems.at[n])
+        for n, (src, dst) in enumerate((
+            (edges_hbm, edges_ref), (w1_hbm, w1_ref), (w2_hbm, w2_ref),
+            (v1_hbm, v1_ref), (v2_hbm, v2_ref), (edge_cot_hbm, edge_cot_ref),
+        ))
+    ]
     barrier = pltpu.get_barrier_semaphore()
     for k in range(1, DEVICES):
         pl.semaphore_signal(
             barrier, inc=1, device_id=flat(k)[1], device_id_type=pl.DeviceIdType.MESH
         )
+    for load in loads:
+        load.start()
     nodes = nodes_ref[...]
     send_row = index_ref[:, 1792:2048]
     outgoing[...] = dot(column_hot(send_row, 0, OWN), nodes).astype(bf16)
@@ -357,20 +366,20 @@
     b1_row, b2_row, gain = params_ref[0:1, :], params_ref[1:2, :], params_ref[2:3, :]
     c1_row, c2_row, node_gain = params_ref[3:4, :], params_ref[4:5, :], params_ref[5:6, :]
 
+    loads[0].wait()
+    loads[1].wait()
     for first, size in PIECES[:3]:
         rows = pl.ds(first, size)
-        joined[rows, 0:512] = edges_ref[rows, :]
         masked[rows, :] = edges_ref[rows, :]
         picker = column_hot(index_ref[:, 896 + first:896 + first + size], 0, OWN)
-        joined[rows, 1024:1536] = dot(picker, nodes).astype(bf16)
+        to_rows = dot(picker, nodes).astype(bf16)
+        before_ref[rows, :] = (
+            dot(edges_ref[rows, :], w1_ref[0:512, :]) + dot(to_rows, w1_ref[1024:1536, :]) + b1_row
+        )
+    loads[2].wait()
     for copy in halo:
         copy.wait()
     extended = ext[...]
-    for first, size in PIECES[:3]:
-        rows = pl.ds(first, size)
-        picker = column_hot(index_ref[:, first:first + size], 0, EXTENDED)
-        joined[rows, 512:1024] = dot(picker, extended).astype(bf16)
-
     piece_rows = lax.broadcasted_iota(jnp.int32, (128, 1), 0)
     is_own = (piece_rows >= 2 * position) & (piece_rows < 2 * position + 2)
     own_mask = jnp.where(is_own, 1.0, 0.0)
@@ -380,34 +389,46 @@
         if first == FINE:
             for copy in coarse:
                 copy.wait()
-            table = coarse_tiles[...].reshape(DEVICES * 16, 512)
-            picked = dot(column_hot(index_ref[:, 2048:2176], 0, DEVICES * 16), table)
+            table = coarse_tiles[...].reshape(DEVICES * 32, 128)
+            picked = jnp.concatenate([
+                dot(column_hot(index_ref[:, 2048:2176] + part, 0, DEVICES * 32), table)
+                for part in range(4)
+            ], axis=1)
             blank = jnp.zeros((96, 512), f32)
 
             def placed(part):
                 return jnp.concatenate([part, blank], axis=0)
 
             latents = placed(picked[0:32])
-            joined[rows, 0:512] = latents.astype(bf16)
-            joined[rows, 512:1024] = placed(picked[32:64]).astype(bf16)
-            joined[rows, 1024:1536] = placed(picked[64:96]).astype(bf16)
+            joined[:, 0:512] = latents.astype(bf16)
+            joined[:, 512:1024] = placed(picked[32:64]).astype(bf16)
+            joined[:, 1024:1536] = placed(picked[64:96]).astype(bf16)
             masked[rows, :] = (latents * own_mask).astype(bf16)
             coarse_cot[...] = placed(picked[96:128])
-        before = dot(joined[rows, :], w1_ref[...]) + b1_row
+            before = dot(joined[...], w1_ref[...]) + b1_row
+        else:
+            picker = column_hot(index_ref[:, first:first + size], 0, EXTENDED)
+            before = before_ref[rows, :] + dot(
+                dot(picker, extended).astype(bf16), w1_ref[512:1024, :]
+            )
         before_ref[rows, :] = before
         hidden = (before * jax.nn.sigmoid(before)).astype(bf16)
         hidden_ref[rows, :] = hidden
         after = dot(hidden, w2_ref[...]) + b2_row
         normed, inv_scale = layer_norm_parts(after)
         normed_ref[rows, :] = normed
+        own_latents = joined[:, 0:512] if first == FINE else edges_ref[rows, :]
         inv_ref[rows, :] = jnp.broadcast_to(inv_scale, (size, 128))
-        updated_ref[rows, :] = (joined[rows, 0:512].astype(f32) + normed * gain).astype(bf16)
+        updated_ref[rows, :] = (own_latents.astype(f32) + normed * gain).astype(bf16)
     coarse_rows = pl.ds(FINE, 128)
     hidden_ref[coarse_rows, :] = (hidden_ref[coarse_rows, :].astype(f32) * own_mask).astype(bf16)
 
     to_receiver = row_hot(index_ref[:, 896:1792], OWN)
     summed = dot(to_receiver, updated_ref[...])
 
+    loads[3].wait()
+    loads[4].wait()
+    loads[5].wait()
     summed_low = summed.astype(bf16)
     node_before = dot(nodes, v1_ref[0:512, :]) + dot(summed_low, v1_ref[512:1024, :]) + c1_row
     sigma = jax.nn.sigmoid(node_before)
@@ -476,22 +497,30 @@
             (group, region, lax.rem(sub + step, SIDE)),
         )
 
+    def pass_on(n, way, block):
+        line_copy(n, way, block).wait_recv()
+        along[n][way, block] = (
+            totals[n][block] + arrived[n][way, block].astype(f32)
+        ).astype(bf16)
+        line_copy(n, way, block).start()
+
+    def line_begin(n):
+        for way, first in ((0, 0), (1, SIDE - 1)):
+            @pl.when(sub == first)
+            def _():
+                for k in range(SIDE - 1):
+                    block = 3 - k if way == 0 else k
+                    along[n][way, block] = totals[n][block].astype(bf16)
+                    line_copy(n, way, block).start()
+
     def line_step(n, k):
-        for way, block, first, sends in (
-            (0, 3 - k, 0, sub < 3 - k), (1, k, SIDE - 1, sub > k)
+        for here, moves in (
+            (1, (((0, 3),), ((0, 2), (1, 0)))), (2, (((1, 0),), ((1, 1), (0, 3))))
         ):
-            @pl.when(sends & (sub == first))
+            @pl.when(sub == here)
             def _():
-                along[n][way, block] = totals[n][block].astype(bf16)
-                line_copy(n, way, block).start()
-
-            @pl.when(sends & (sub != first))
-            def _():
-                line_copy(n, way, block).wait_recv()
-                along[n][way, block] = (
-                    totals[n][block] + arrived[n][way, block].astype(f32)
-                ).astype(bf16)
-                line_copy(n, way, block).start()
+                for way, block in moves[k]:
+                    pass_on(n, way, block)
 
     def line_end(n):
         @pl.when(sub > 0)
@@ -577,7 +606,6 @@
         )
         copy.start()
         back.append(copy)
-    start_column(1)
     for n, buffer in ((2, g2), (3, g3)):
         cols = slice(256 * (n - 2), 256 * (n - 2) + 256)
         inner = jnp.concatenate([
@@ -588,36 +616,50 @@
         buffer[...] = inner.astype(bf16).reshape(buffer.shape)
         start_core(n)
         if n == 2:
-            total_column(0)
-            line_step(0, 0)
+            start_column(1)
     start_column(2)
-    line_step(0, 1)
-    start_column(3)
+    total_column(0)
+    line_begin(0)
     own = node_direct + from_grads[0:OWN]
     own = own + (contract_cols(to_high, w1c) + contract_cols(to_low, w1c))
-    line_step(0, 2)
+    start_column(3)
+    line_step(0, 0)
+    total_column(1)
+    line_begin(1)
+    line_step(0, 1)
     for copy in back:
         copy.wait()
     own = own + dot(row_hot(send_row, OWN), returned[...])
     grad_nodes_ref[...] = own.astype(bf16)
-    total_column(1)
     line_step(1, 0)
+    total_column(2)
+    line_begin(2)
     line_step(1, 1)
-    line_step(1, 2)
-    total_column(2)
-    line_step(2, 0)
     node_block = line_end(0)
     out_ni_ref[...] = node_block[0:64]
     out_no_ref[...] = node_block[64:96]
+    line_step(2, 0)
+    total_column(3)
+    line_begin(3)
     line_step(2, 1)
-    total_column(3)
+    out_eo_ref[...] = line_end(1)
     line_step(3, 0)
-    line_step(2, 2)
     line_step(3, 1)
-    out_eo_ref[...] = line_end(1)
-    line_step(3, 2)
     out_ei_ref[:, 0:256] = line_end(2)
     out_ei_ref[:, 256:512] = line_end(3)
+
+
+def hand_over(*refs):
+    held, sems = refs[14:21], refs[21]
+    inward = [pltpu.make_async_copy(refs[n], held[n], sems.at[0, n]) for n in range(7)]
+    outward = [pltpu.make_async_copy(held[n], refs[7 + n], sems.at[1, n]) for n in range(7)]
+    for copy in inward:
+        copy.start()
+    for n in range(7):
+        inward[n].wait()
+        outward[n].start()
+    for copy in outward:
+        copy.wait()
 
 
 def fused_device(
@@ -632,12 +674,12 @@
     padded_sender = edge_sender + halo_slot * (SLOT - send_list.shape[2])
     none = jnp.full((96,), -1, jnp.int32)
     every = jnp.arange(2 * DEVICES, dtype=jnp.int32)
-    tile_row = 16 * (every // 2) + every % 2
+    tile_row = 32 * (every // 2) + 4 * (every % 2)
     index = jnp.concatenate([
         padded_sender, jnp.where(coarse_sender == position, 0, -1), none,
         edge_receiver, jnp.where(coarse_receiver == position, 0, -1), none,
         jnp.pad(send_list[0], ((0, 0), (0, SLOT - send_list.shape[2])), constant_values=-1).reshape(-1),
-        tile_row + 1, 16 * coarse_sender, 16 * coarse_receiver, tile_row + 3,
+        tile_row + 4, 32 * coarse_sender, 32 * coarse_receiver, tile_row + 12,
         coarse_receiver, none,
     ]).reshape(1, -1)
     blank = jnp.zeros((512,), f32)
@@ -646,17 +688,24 @@
         node_inner_bias, node_outer_bias, node_gain, blank, blank,
     ])
     packet = jnp.concatenate(
-        [node_latents[:1], coarse_latents, coarse_cotangent, jnp.zeros((11, 512), bf16)], axis=0
-    )
+        [node_latents[:1], coarse_latents, coarse_cotangent, jnp.zeros((3, 512), bf16)], axis=0
+    ).reshape(32, 128)
 
     def per_chunk(make):
         return [pltpu.VMEM(*make(rows, cols)) for rows, cols in CHUNKS]
 
     scratch = [
-        pltpu.VMEM((ROWS, 1536), bf16),
+        pltpu.VMEM((FINE, 512), bf16),
+        pltpu.VMEM((FINE, 512), bf16),
+        pltpu.VMEM((1536, 512), bf16),
+        pltpu.VMEM((512, 512), bf16),
+        pltpu.VMEM((1024, 512), bf16),
+        pltpu.VMEM((512, 512), bf16),
+        dma((6,)),
+        pltpu.VMEM((128, 1536), bf16),
         pltpu.VMEM((EXTENDED, 512), bf16),
         pltpu.VMEM((8 * SLOT, 512), bf16),
-        pltpu.VMEM((DEVICES, 16, 512), bf16),
+        pltpu.VMEM((DEVICES, 32, 128), bf16),
         pltpu.VMEM((ROWS, 512), f32),
         pltpu.VMEM((ROWS, 512), bf16),
         pltpu.VMEM((ROWS, 512), f32),
@@ -682,13 +731,14 @@
     ]
     shape = jax.ShapeDtypeStruct
     vmem = pl.BlockSpec(memory_space=pltpu.VMEM)
-    return pl.pallas_call(
+    hbm = pl.BlockSpec(memory_space=pl.ANY)
+    results = pl.pallas_call(
         step_kernel,
         out_shape=(
             shape((OWN, 512), bf16), shape((FINE, 512), bf16), shape((2, 512), bf16),
             shape((96, 512), f32), shape((32, 512), f32), shape((64, 512), f32), shape((32, 512), f32),
         ),
-        in_specs=[vmem] * 11,
+        in_specs=[vmem] * 4 + [hbm, vmem] + [hbm] * 5,
         out_specs=(vmem,) * 7,
         scratch_shapes=scratch,
         compiler_params=pltpu.CompilerParams(
@@ -698,6 +748,13 @@
         index, params, packet, node_latents, edge_latents, node_cotangent, edge_cotangent,
         edge_inner, edge_outer, node_inner, node_outer,
     )
+    return pl.pallas_call(
+        hand_over,
+        out_shape=tuple(shape(result.shape, result.dtype) for result in results),
+        in_specs=[hbm] * 7,
+        out_specs=(hbm,) * 7,
+        scratch_shapes=[pltpu.VMEM(result.shape, result.dtype) for result in results] + [dma((2, 7))],
+    )(*results)
 
 
 def solution(mesh):

time: 90.9 us -> 68.2 us (0.75)
  Pallas kernels: 75.9 us -> 60 us
  local copies, waits for them, and re-layouts: 11.2 us -> 4.94 us
    pallas_call x1, Pallas kernels: 75.9 us -> 57.6 us  [fused_device(): pl.pallas_call(step_kernel, out_shape=(shape((OWN, 512), bf16), shape((FI...]
    unnamed x17 -> x0, local copies, waits for them, and re-layouts: 6.88 us -> none
    pallas_call x0 -> x1, Pallas kernels: none -> 2.36 us  [fused_device(): pl.pallas_call(hand_over, out_shape=tuple((shape(result.shape, result.dty...]
where the time goes in v2:
time: 68.2 us; the launch traced here: 67.7 us
  Pallas kernels  60 us (88%)
  local copies, waits for them, and re-layouts  4.94 us (7%)
  other arithmetic  2.15 us (3%)
    pallas_call x1, Pallas kernels, fused_device(): pl.pallas_call(step_kernel, out_shape=(shape((OWN, 512), bf16), shape((FI...  57.6 us
    pallas_call x1, Pallas kernels, fused_device(): pl.pallas_call(hand_over, out_shape=tuple((shape(result.shape, result.dty...  2.36 us
    another operation x2, local copies, waits for them, and re-layouts, fused_device(): jnp.stack([edge_inner_bias, edge_outer_bias, edge_gain, node_inner_bias,...  1.39 us

profile of v2, /device:TPU:0, one launch (start us, length us, event | category | flops | bytes accessed | tf_op | source)
XLA Modules:
  0.0 67.7 jit_solution(3282679319484408510)
XLA Ops:
  0.6 0.1 pad.8.clone
  0.7 0.7 broadcast_multiply_fusion
  1.4 0.7 %slice.3 = bf16[1,512]{1,0:T(2,128)(2,1)S(1)} slice(bf16[128,512]{1,0:T(8,128)(2,1)} %nodes_ref.1), slice={[0:1], [0:512]} | slice | bytes 2048 | tf_op jit(solution)/shard_map/slice | solution.py:691
  2.1 0.7 %pad.4 = s32[8,32]{1,0:T(8,128)S(1)} pad(s32[8,24]{1,0:T(8,128)} %bitcast.7, s32[]{:T(128)} %constant.54.clone.1), padding=0_0x0_8 | pad | bytes 1796 | tf_op jit(solution)/shard_map/jit(_pad)/pad | solution.py:681
  2.8 0.1 reshape.23
  2.9 0.7 %fusion.1 = s32[768]{0:T(1024)S(1)} fusion(s32[768]{0:T(1024)} %param.38), kind=kLoop, calls=%fused_computation.3 | loop fusion | flops 9216 | bytes 6144 | tf_op jit(solution)/shard_map/add | solution.py:674
  3.6 0.8 %concatenate.6 = s32[2304]{0:T(1024)S(1)} concatenate(s32[768]{0:T(1024)S(1)} %fusion.1, s32[32]{0:T(128)S(1)} %get-tuple-element.25, s32[96]{0:T(128)S(1)} %broadcast_in_dim.18, s32[768]{0:T(1024)} %param.39, s32[32]{0:T(128)S(1)} %get-tuple-element.22, s32[96]{0:T(128)S(1)} %broadcast_in_dim.18, s32[256]{0:T(256)S(1)} %reshape.23, s32[32]{0:T(128)S(1)} %get-tuple-element.28, ...), dimensions={0} | concatenate | bytes 18432 | tf_op jit(solution)/shard_map/concatenate | solution.py:678
  4.4 0.6 reshape.24.index_ref
  5.0 0.8 %maximum_maximum_fusion = bf16[8,512]{1,0:T(8,128)(2,1)S(1)} fusion(bf16[2,512]{1,0:T(2,128)(2,1)} %param.26, bf16[2,512]{1,0:T(2,128)(2,1)} %param.23, bf16[1,512]{1,0:T(2,128)(2,1)S(1)} %slice.3, bf16[8]{0:T(256)(128)(2,1)S(1)} %pad.8.clone), kind=kLoop, calls=%fused_computation | loop fusion | flops 32768 | bytes 13328 | tf_op jit(solution)/shard_map/concatenate | solution.py:690
  5.7 0.6 reshape.25.packet_ref
  6.4 1.4 %stack.31.params_ref = f32[8,512]{1,0:T(8,128)} concatenate(f32[1,512]{1,0:T(1,128)} %bitcast.8, f32[1,512]{1,0:T(1,128)} %bitcast.9, f32[1,512]{1,0:T(1,128)} %bitcast.10, f32[1,512]{1,0:T(1,128)} %bitcast.11, f32[1,512]{1,0:T(1,128)} %bitcast.12, f32[1,512]{1,0:T(1,128)} %bitcast.13, f32[2,512]{1,0:T(2,128)S(1)} %stack.30), dimensions={0} | concatenate | bytes 32768 | tf_op jit(solution)/shard_map/stack | solution.py:686
  7.8 57.6 %shard_map.252 = (bf16[128,512]{1,0:T(8,128)(2,1)}, bf16[768,512]{1,0:T(8,128)(2,1)}, bf16[2,512]{1,0:T(2,128)(2,1)}, f32[96,512]{1,0:T(8,128)}, f32[32,512]{1,0...) custom-call(s32[1,2304]{1,0:T(1,128)} %reshape.24.index_ref, f32[8,512]{1,0:T(8,128)} %stack.31.params_ref, ...), custom_call_target="tpu_custom_call" | custom-call | tf_op jit(solution)/shard_map/pallas_call | solution.py:735
  65.4 2.4 %shard_map.253 = (bf16[128,512]{1,0:T(8,128)(2,1)}, bf16[768,512]{1,0:T(8,128)(2,1)}, bf16[2,512]{1,0:T(2,128)(2,1)}, f32[96,512]{1,0:T(8,128)}, f32[32,512]{1,0...) custom-call(bf16[128,512]{1,0:T(8,128)(2,1)} %get-tuple-element.14.refs_0_, bf16[768,512]{1,0:T(8,128)(2,1)} %get-tuple-element.15.refs_1_, ...), custom_call_target="tpu_custom_call" | custom-call | tf_op jit(solution)/shard_map/pallas_call | solution.py:751
  (4 shorter events, 0.0 us)

commit v3 on v2

--- a/solution.py
+++ b/solution.py
@@ -285,7 +285,7 @@
 
 
 def step_kernel(
-    index_ref, params_ref, packet_ref,
+    index_ref, p0, p1, p2, p3, p4, p5, coarse_lat_ref, coarse_cot_in, from_ref, into_ref,
     nodes_ref, edges_hbm, node_cot_ref, edge_cot_hbm, w1_hbm, w2_hbm, v1_hbm, v2_hbm,
     grad_nodes_ref, grad_edges_ref, grad_coarse_ref,
     out_ei_ref, out_eo_ref, out_ni_ref, out_no_ref,
@@ -334,9 +334,19 @@
     for load in loads:
         load.start()
     nodes = nodes_ref[...]
-    send_row = index_ref[:, 1792:2048]
+    send_row = index_ref[:, 256:512]
     outgoing[...] = dot(column_hot(send_row, 0, OWN), nodes).astype(bf16)
-    coarse_tiles[position] = packet_ref[...]
+    tile_rows = lax.broadcasted_iota(jnp.int32, (32, 128), 0)
+    tile = jnp.zeros((32, 128), f32)
+    packed = (
+        nodes_ref[0:16, :].astype(f32)[0:1],
+        *(coarse_lat_ref[...].astype(f32)[j:j + 1] for j in range(2)),
+        *(coarse_cot_in[...].astype(f32)[j:j + 1] for j in range(2)),
+    )
+    for n, row in enumerate(packed):
+        for part in range(4):
+            tile = jnp.where(tile_rows == 4 * n + part, row[:, 128 * part:128 * part + 128], tile)
+    coarse_tiles[position] = tile.astype(bf16)
     ext[0:OWN, :] = nodes
     pl.semaphore_wait(barrier, DEVICES - 1)
 
@@ -363,15 +373,20 @@
             coarse_send.at[k], coarse_recv.at[k], device,
         ))
 
-    b1_row, b2_row, gain = params_ref[0:1, :], params_ref[1:2, :], params_ref[2:3, :]
-    c1_row, c2_row, node_gain = params_ref[3:4, :], params_ref[4:5, :], params_ref[5:6, :]
+    b1_row, b2_row, gain, c1_row, c2_row, node_gain = (
+        vector[...].reshape(1, 512) for vector in (p0, p1, p2, p3, p4, p5)
+    )
+    from_row = from_ref[...].reshape(1, FINE)
+    receiver = into_ref[...].reshape(1, FINE)
+    slot_of = lax.shift_right_logical(jnp.maximum(from_row - OWN, 0) * 2731, 16)
+    from_row = from_row + 8 * slot_of
 
     loads[0].wait()
     loads[1].wait()
     for first, size in PIECES[:3]:
         rows = pl.ds(first, size)
         masked[rows, :] = edges_ref[rows, :]
-        picker = column_hot(index_ref[:, 896 + first:896 + first + size], 0, OWN)
+        picker = column_hot(receiver[:, first:first + size], 0, OWN)
         to_rows = dot(picker, nodes).astype(bf16)
         before_ref[rows, :] = (
             dot(edges_ref[rows, :], w1_ref[0:512, :]) + dot(to_rows, w1_ref[1024:1536, :]) + b1_row
@@ -391,7 +406,7 @@
                 copy.wait()
             table = coarse_tiles[...].reshape(DEVICES * 32, 128)
             picked = jnp.concatenate([
-                dot(column_hot(index_ref[:, 2048:2176] + part, 0, DEVICES * 32), table)
+                dot(column_hot(index_ref[:, 512:640] + part, 0, DEVICES * 32), table)
                 for part in range(4)
             ], axis=1)
             blank = jnp.zeros((96, 512), f32)
@@ -407,7 +422,7 @@
             coarse_cot[...] = placed(picked[96:128])
             before = dot(joined[...], w1_ref[...]) + b1_row
         else:
-            picker = column_hot(index_ref[:, first:first + size], 0, EXTENDED)
+            picker = column_hot(from_row[:, first:first + size], 0, EXTENDED)
             before = before_ref[rows, :] + dot(
                 dot(picker, extended).astype(bf16), w1_ref[512:1024, :]
             )
@@ -423,7 +438,7 @@
     coarse_rows = pl.ds(FINE, 128)
     hidden_ref[coarse_rows, :] = (hidden_ref[coarse_rows, :].astype(f32) * own_mask).astype(bf16)
 
-    to_receiver = row_hot(index_ref[:, 896:1792], OWN)
+    to_receiver = row_hot(jnp.concatenate([receiver, index_ref[:, 128:256]], axis=1), OWN)
     summed = dot(to_receiver, updated_ref[...])
 
     loads[3].wait()
@@ -561,10 +576,10 @@
             gathered = jnp.concatenate([coarse_sums[:, part, :] for part in range(4)], axis=1)
             gathered = jnp.concatenate([gathered, jnp.zeros((OWN - DEVICES, 512), f32)], axis=0)
             high, low = two_parts(gathered)
-            picker = column_hot(index_ref[:, 2176:2304], 0, OWN)
+            picker = column_hot(index_ref[:, 640:768], 0, OWN)
             total = coarse_cot[...] + (dot(picker, high) + dot(picker, low))
         else:
-            picker = column_hot(index_ref[:, 896 + first:896 + first + size], 0, OWN)
+            picker = column_hot(receiver[:, first:first + size], 0, OWN)
             total = edge_cot_ref[rows, :].astype(f32) + (dot(picker, sums_high) + dot(picker, sums_low))
         after_low = gradient_after(
             total, gain, normed_ref[rows, :], inv_ref[rows, 0:1]
@@ -591,7 +606,7 @@
 
     g1[...] = contract_rows(hidden_ref[...], after_low_ref[...]).astype(bf16).reshape(g1.shape)
     start_core(1)
-    to_sender = row_hot(index_ref[:, 0:896], EXTENDED)
+    to_sender = row_hot(jnp.concatenate([from_row, index_ref[:, 0:128]], axis=1), EXTENDED)
     from_high, from_low = two_parts(dot(to_sender, before_low_ref[...]))
     to_high, to_low = two_parts(dot(to_receiver, before_low_ref[...]))
     w1b, w1c = w1_ref[512:1024, :], w1_ref[1024:1536, :]
@@ -670,27 +685,16 @@
 ):
     bf16, f32, dma = jnp.bfloat16, jnp.float32, pltpu.SemaphoreType.DMA
     position = lax.axis_index("region") * SIDE + lax.axis_index("sub")
-    halo_slot = jnp.maximum(edge_sender - OWN, 0) // send_list.shape[2]
-    padded_sender = edge_sender + halo_slot * (SLOT - send_list.shape[2])
     none = jnp.full((96,), -1, jnp.int32)
     every = jnp.arange(2 * DEVICES, dtype=jnp.int32)
     tile_row = 32 * (every // 2) + 4 * (every % 2)
     index = jnp.concatenate([
-        padded_sender, jnp.where(coarse_sender == position, 0, -1), none,
-        edge_receiver, jnp.where(coarse_receiver == position, 0, -1), none,
+        jnp.where(coarse_sender == position, 0, -1), none,
+        jnp.where(coarse_receiver == position, 0, -1), none,
         jnp.pad(send_list[0], ((0, 0), (0, SLOT - send_list.shape[2])), constant_values=-1).reshape(-1),
         tile_row + 4, 32 * coarse_sender, 32 * coarse_receiver, tile_row + 12,
         coarse_receiver, none,
     ]).reshape(1, -1)
-    blank = jnp.zeros((512,), f32)
-    params = jnp.stack([
-        edge_inner_bias, edge_outer_bias, edge_gain,
-        node_inner_bias, node_outer_bias, node_gain, blank, blank,
-    ])
-    packet = jnp.concatenate(
-        [node_latents[:1], coarse_latents, coarse_cotangent, jnp.zeros((3, 512), bf16)], axis=0
-    ).reshape(32, 128)
-
     def per_chunk(make):
         return [pltpu.VMEM(*make(rows, cols)) for rows, cols in CHUNKS]
 
@@ -738,14 +742,16 @@
             shape((OWN, 512), bf16), shape((FINE, 512), bf16), shape((2, 512), bf16),
             shape((96, 512), f32), shape((32, 512), f32), shape((64, 512), f32), shape((32, 512), f32),
         ),
-        in_specs=[vmem] * 4 + [hbm, vmem] + [hbm] * 5,
+        in_specs=[vmem] * 12 + [hbm, vmem] + [hbm] * 5,
         out_specs=(vmem,) * 7,
         scratch_shapes=scratch,
         compiler_params=pltpu.CompilerParams(
             collective_id=0, has_side_effects=True, vmem_limit_bytes=58 * 2**20
         ),
     )(
-        index, params, packet, node_latents, edge_latents, node_cotangent, edge_cotangent,
+        index, edge_inner_bias, edge_outer_bias, edge_gain,
+        node_inner_bias, node_outer_bias, node_gain, coarse_latents, coarse_cotangent,
+        edge_sender, edge_receiver, node_latents, edge_latents, node_cotangent, edge_cotangent,
         edge_inner, edge_outer, node_inner, node_outer,
     )
     return pl.pallas_call(

time: 68.2 us -> 63.8 us (0.935)
  local copies, waits for them, and re-layouts: 4.94 us -> 2.09 us
  other arithmetic: 2.15 us -> 0.69 us
    another operation x2 -> x0, local copies, waits for them, and re-layouts: 1.39 us -> none  [fused_device(): jnp.stack([edge_inner_bias, edge_outer_bias, edge_gain, node_inner_bias,...]
    concatenate x1 -> x0, other arithmetic: 0.77 us -> none  [fused_device(): jnp.concatenate([node_latents[:1], coarse_latents, coarse_cotangent, jnp....]
    add x1 -> x0, other arithmetic: 0.7 us -> none  [fused_device(): padded_sender = edge_sender + halo_slot * (SLOT - send_list.shape[2])]
    slice x1 -> x0, local copies, waits for them, and re-layouts: 0.7 us -> none  [fused_device(): node_latents[:1]]
where the time goes in v3:
time: 63.8 us; the launch traced here: 63.5 us
  Pallas kernels  60.1 us (94%)
  local copies, waits for them, and re-layouts  2.09 us (3%)
  other arithmetic  0.69 us (1%)
  between operations  0.65 us (1%)
    pallas_call x1, Pallas kernels, fused_device(): pl.pallas_call(step_kernel, out_shape=(shape((OWN, 512), bf16), shape((FI...  57.8 us
    pallas_call x1, Pallas kernels, fused_device(): pl.pallas_call(hand_over, out_shape=tuple((shape(result.shape, result.dty...  2.36 us

profile of v3, /device:TPU:0, one launch (start us, length us, event | category | flops | bytes accessed | tf_op | source)
XLA Modules:
  0.0 63.5 jit_solution(17655701612201253066)
XLA Ops:
  0.6 0.7 %broadcast_multiply_fusion = (s32[32]{0:T(128)S(1)}, s32[32]{0:T(128)S(1)}, s32[32]{0:T(128)S(1)}, s32[32]{0:T(128)S(1)}) fusion(s32[32]{0:T(128)} %param.41, s32[]{:T(128)S(6)} %add.28, s32[32]{0:T(128)} %param.40), kind=kLoop, calls=%fused_computation.12 | loop fusion | flops 192 | bytes 772 | tf_op jit(solution)/shard_map/mul | solution.py:695
  1.3 0.7 %pad.4 = s32[8,32]{1,0:T(8,128)S(1)} pad(s32[8,24]{1,0:T(8,128)} %bitcast.1, s32[]{:T(128)} %constant.41.clone.1), padding=0_0x0_8 | pad | bytes 1796 | tf_op jit(solution)/shard_map/jit(_pad)/pad | solution.py:694
  2.0 0.1 reshape.20
  2.1 0.7 %concatenate.3 = s32[768]{0:T(1024)S(1)} concatenate(s32[32]{0:T(128)S(1)} %get-tuple-element.25, s32[96]{0:T(128)S(1)} %broadcast_in_dim.15, s32[32]{0:T(128)S(1)} %get-tuple-element.22, s32[96]{0:T(128)S(1)} %broadcast_in_dim.15, s32[256]{0:T(256)S(1)} %reshape.20, s32[32]{0:T(128)S(1)} %get-tuple-element.28, s32[32]{0:T(128)S(1)} %get-tuple-element.26, ...), dimensions={0} | concatenate | bytes 6144 | tf_op jit(solution)/shard_map/concatenate | solution.py:691
  2.8 0.6 reshape.21.index_ref
  3.4 57.8 %shard_map.252 = (bf16[128,512]{1,0:T(8,128)(2,1)}, bf16[768,512]{1,0:T(8,128)(2,1)}, bf16[2,512]{1,0:T(2,128)(2,1)}, f32[96,512]{1,0:T(8,128)}, f32[32,512]{1,0...) custom-call(s32[1,768]{1,0:T(1,128)} %reshape.21.index_ref, f32[512]{0:T(512)} %p0.1, f32[512]{0:T(512)} %p1.1, f32[512]{0:T(512)} %p2.1, ...), custom_call_target="tpu_custom_call" | custom-call | tf_op jit(solution)/shard_map/pallas_call | solution.py:739
  61.2 2.4 %shard_map.253 = (bf16[128,512]{1,0:T(8,128)(2,1)}, bf16[768,512]{1,0:T(8,128)(2,1)}, bf16[2,512]{1,0:T(2,128)(2,1)}, f32[96,512]{1,0:T(8,128)}, f32[32,512]{1,0...) custom-call(bf16[128,512]{1,0:T(8,128)(2,1)} %get-tuple-element.14.refs_0_, bf16[768,512]{1,0:T(8,128)(2,1)} %get-tuple-element.15.refs_1_, ...), custom_call_target="tpu_custom_call" | custom-call | tf_op jit(solution)/shard_map/pallas_call | solution.py:757
  (2 shorter events, 0.0 us)
